TPU v7x, 32 devices: a whole 2x2x4 slice. The times are simulated.
32 devices in a mesh: seq: 8 (over z, y), mp: 4 (over x, core).
Axes of the slice: x: 2, y: 2, z: 4, core: 2. Of those that a mesh axis runs over, the one named last changes fastest.
Arguments:
- queries: bfloat16 [4096, 8192], P('seq', 'mp'), may hold values from -6 to 6
- keys_in: bfloat16 [4096, 8192], P('seq', 'mp'), may hold values from -6 to 6
- values_in: bfloat16 [4096, 8192], P('seq', 'mp'), may hold values from -6 to 6
- residual: bfloat16 [4096, 8192], P('seq', 'mp')
- short_taps: bfloat16 [3, 7, 8192], P(None, None, 'mp'), may hold values from -2 to 2
- mr_filter: bfloat16 [128, 512], P('seq', 'mp'), may hold values from -0.5 to 0.5
- norm_gain: bfloat16 [8192], P('mp'), may hold values from 0.5 to 1.5
- predecessor: int32 [8], replicated, may hold values from -1 to 7, as said below
- stretch_lengths: int32 [8], replicated, may hold values from 1 to 512, as said below
Outputs:
- mixed: bfloat16 [4096, 8192], P('seq', 'mp')
- normed: bfloat16 [4096, 8192], P('seq', 'mp')
Inputs may be any that keep to these rules, and one draw needn't show every extreme that they name: predecessor[j] is the stretch holding the preceding 512 tokens of stretch j's genome, or -1 for a genome's first stretch; each stretch precedes at most one stretch, and the chains have no cycles. `stretch_lengths`: every stretch that precedes another stretch is full (512 valid tokens); valid tokens come first.
All inputs are finite; a program needn't handle non-finite values.
Results may differ from a plain program's by a relative error of at most 0.0049.
Values may be sent and summed in bfloat16 or wider, within the bound.
No kernel may reach another device: no remote copies, remote signals or barrier semaphores. Data moves between devices by JAX's collectives and lax.ppermute only.
A program may use at most 64 MiB of HBM per device.

v0:
```python
import functools

import jax
import jax.numpy as jnp
from jax import lax
from jax.experimental import pallas as pl
from jax.experimental.pallas import tpu as pltpu
from jax.sharding import PartitionSpec as P

EPSILON = 1e-06
F32 = jnp.float32
BF16 = jnp.bfloat16
LANES = 128
STEP = 256
WIDE = 512
BLOCK = 32
WINDOW = 256
PACKED = 160
OPENING = 144
VMEM_LIMIT = 64 * 1024 * 1024


def params():
    return pltpu.CompilerParams(vmem_limit_bytes=VMEM_LIMIT)


def cost(flops, bytes_accessed):
    return pl.CostEstimate(flops=flops, bytes_accessed=bytes_accessed, transcendentals=0)


def short_conv(scratch, taps, start, rows):
    total = None
    for offset in range(taps.shape[0]):
        term = taps[offset : offset + 1] * scratch[pl.ds(start + 8 - offset, rows), :]
        total = term if total is None else total + term
    return total


def tail_kernel(packed, q_ref, k_ref, v_ref, kb_ref, vb_ref, taps_ref, filt_ref, out_ref, ks, vs):
    def piece(slot, carry):
        lasts = []
        for tile in range(STEP // LANES):
            cols = pl.ds(pl.multiple_of(slot * STEP + tile * LANES, LANES), LANES)
            here = slice(tile * LANES, (tile + 1) * LANES)
            kt, vt = ks.at[tile], vs.at[tile]
            kt[0:16, :] = kb_ref[:, cols].astype(F32)
            vt[0:16, :] = vb_ref[:, cols].astype(F32)
            kt[16:144, :] = k_ref[:, cols].astype(F32)
            vt[16:144, :] = v_ref[:, cols].astype(F32)
            key_taps = taps_ref[1, :, cols].astype(F32)
            value_taps = taps_ref[2, :, cols].astype(F32)
            for row in range(0, 128, 64):
                key = short_conv(kt, key_taps, row + 8, 64)
                value = short_conv(vt, value_taps, row + 8, 64)
                out_ref[slot, row : row + 64, here] = (key * value).astype(BF16)
            last = [q_ref[:, cols].astype(F32)[8:], kt[136:144, :], vt[136:144, :]]
            if packed:
                last.append(filt_ref[...].astype(F32)[8 * tile : 8 * tile + 8])
            else:
                last.append(jnp.zeros((8, LANES), F32))
            lasts.append(jnp.concatenate(last))
        out_ref[slot, 128:PACKED, :] = jnp.concatenate(lasts, axis=1).astype(BF16)
        return carry

    lax.fori_loop(0, out_ref.shape[0], piece, 0)


def tail_call(packed, queries, keys_in, values_in, short_taps, mr_filter):
    rows, width = queries.shape
    slots = width // STEP
    return pl.pallas_call(
        functools.partial(tail_kernel, packed),
        grid=(1,),
        in_specs=[
            pl.BlockSpec((16, width), lambda p: (rows // 16 - 1, 0)),
            pl.BlockSpec((128, width), lambda p: (rows // 128 - 1, 0)),
            pl.BlockSpec((128, width), lambda p: (rows // 128 - 1, 0)),
            pl.BlockSpec((16, width), lambda p: (rows // 16 - 9, 0)),
            pl.BlockSpec((16, width), lambda p: (rows // 16 - 9, 0)),
            pl.BlockSpec(short_taps.shape, lambda p: (0, 0, 0)),
            pl.BlockSpec(mr_filter.shape, lambda p: (0, 0)),
        ],
        out_specs=pl.BlockSpec((slots, PACKED, STEP), lambda p: (0, 0, 0)),
        out_shape=jax.ShapeDtypeStruct((slots, PACKED, STEP), BF16),
        scratch_shapes=[pltpu.VMEM((2, 144, LANES), F32), pltpu.VMEM((2, 144, LANES), F32)],
        compiler_params=params(),
        cost_estimate=cost(128 * width * 30, 128 * width * 6),
        name="tail",
    )(queries, keys_in, values_in, keys_in, values_in, short_taps, mr_filter)


def feature_kernel(k_ref, v_ref, taps_ref, out_ref, ks, vs):
    rows = k_ref.shape[0]

    def pair(index, carry):
        for tile in range(2):
            cols = pl.ds(pl.multiple_of(index * 2 * LANES + tile * LANES, LANES), LANES)
            kt, vt = ks.at[tile], vs.at[tile]
            kt[0:8, :] = jnp.zeros((8, LANES), F32)
            vt[0:8, :] = jnp.zeros((8, LANES), F32)
            kt[8 : rows + 8, :] = k_ref[:, cols].astype(F32)
            vt[8 : rows + 8, :] = v_ref[:, cols].astype(F32)
            key_taps = taps_ref[1, :, cols].astype(F32)
            value_taps = taps_ref[2, :, cols].astype(F32)
            for row in range(0, rows, 64):
                key = short_conv(kt, key_taps, row, 64)
                value = short_conv(vt, value_taps, row, 64)
                out_ref[row : row + 64, cols] = (key * value).astype(BF16)
        return carry

    lax.fori_loop(0, k_ref.shape[1] // (2 * LANES), pair, 0)


def feature_call(keys_in, values_in, short_taps):
    rows, width = keys_in.shape
    block = pl.BlockSpec((rows, WIDE), lambda p: (0, p))
    return pl.pallas_call(
        feature_kernel,
        grid=(width // WIDE,),
        in_specs=[block, block, pl.BlockSpec((3, 7, WIDE), lambda p: (0, 0, p))],
        out_specs=block,
        out_shape=jax.ShapeDtypeStruct((rows, width), BF16),
        scratch_shapes=[pltpu.VMEM((2, rows + 8, LANES), F32), pltpu.VMEM((2, rows + 8, LANES), F32)],
        compiler_params=params(),
        cost_estimate=cost(rows * width * 30, rows * width * 6),
        name="features",
    )(keys_in, values_in, short_taps)


def route_kernel(pred_ref, in_ref, out_ref, sems):
    copies = []
    for j in range(in_ref.shape[0]):
        source = jnp.maximum(pred_ref[j], 0)
        copies.append(pltpu.make_async_copy(in_ref.at[source], out_ref.at[j], sems.at[j]))
        copies[-1].start()
    for copy in copies:
        copy.wait()


def route_call(predecessor, received):
    return pl.pallas_call(
        route_kernel,
        in_specs=[pl.BlockSpec(memory_space=pltpu.SMEM), pl.BlockSpec(memory_space=pl.ANY)],
        out_specs=pl.BlockSpec(memory_space=pltpu.VMEM),
        out_shape=jax.ShapeDtypeStruct(received.shape, BF16),
        scratch_shapes=[pltpu.SemaphoreType.DMA((received.shape[0],))],
        compiler_params=params(),
        cost_estimate=cost(0, received.size * 4),
        name="route",
    )(predecessor, received)


def all_taps(filt_ref):
    if len(filt_ref.shape) == 2:
        return filt_ref[...]
    rows = []
    for j in range(filt_ref.shape[0]):
        last = filt_ref[j].astype(F32)[8:]
        rows += [last[:, :LANES], last[:, LANES:]]
    return jnp.concatenate(rows).astype(BF16)


def spread_taps(filter_rows):
    shape = (filter_rows.shape[0], WINDOW)
    tap = lax.broadcasted_iota(jnp.int32, shape, 0)
    place = lax.broadcasted_iota(jnp.int32, shape, 1)
    onehot = (place == WINDOW - BLOCK - tap).astype(BF16)
    return lax.dot_general(filter_rows, onehot, (((0,), (0,)), ((), ())), preferred_element_type=F32)


def toeplitz(lines):
    blocks = []
    for g in range(lines.shape[0]):
        line = jnp.broadcast_to(lines[g : g + 1], (BLOCK, WINDOW))
        blocks.append(pltpu.roll(line, 0, 1, stride=1, stride_axis=0).astype(BF16))
    return jnp.concatenate(blocks)


def pick_groups(result, group_size, rows=BLOCK):
    shape = (rows, result.shape[1])
    group = (lax.broadcasted_iota(jnp.int32, shape, 1) & (LANES - 1)) // group_size
    picked = result[:rows]
    for g in range(1, LANES // group_size):
        picked = jnp.where(group == g, result[g * rows : (g + 1) * rows], picked)
    return picked


def main_kernel(group_size, len_ref, q_ref, u_ref, res_ref, taps_ref, filt_ref, mixed_ref, sum_ref, lines_ref, qs, acc):
    step = pl.program_id(0)
    rows = q_ref.shape[0]
    per_lane = LANES // group_size
    length = len_ref[lax.axis_index("seq")]

    @pl.when(step == 0)
    def _():
        lines_ref[...] = spread_taps(all_taps(filt_ref))
        acc[...] = jnp.zeros_like(acc)

    mixed_ref[0:128, :] = jnp.zeros((128, WIDE), BF16)

    def pair(index, carry):
        for tile in range(2):
            number = index * 2 + tile
            cols = pl.ds(pl.multiple_of(number * LANES, LANES), LANES)
            qt = qs.at[tile]
            qt[0:8, :] = jnp.zeros((8, LANES), F32)
            qt[8 : rows + 8, :] = q_ref[:, cols].astype(F32)
            query_taps = taps_ref[0, :, cols].astype(F32)
            base = pl.multiple_of((step * (WIDE // LANES) + number) * per_lane, per_lane)
            matrix = toeplitz(lines_ref[pl.ds(base, per_lane), :])
            for start in range(128, rows, 2 * BLOCK):
                windows = []
                for first in (start, start + BLOCK):
                    low = first + BLOCK - WINDOW
                    if low < 0:
                        windows.append(
                            jnp.concatenate([jnp.zeros((-low, LANES), BF16), u_ref[0 : first + BLOCK, cols]])
                        )
                    else:
                        windows.append(u_ref[low : first + BLOCK, cols])
                result = jnp.dot(matrix, jnp.concatenate(windows, axis=1), preferred_element_type=F32)
                picked = pick_groups(result, group_size)
                filtered = jnp.concatenate([picked[:, :LANES], picked[:, LANES:]])
                query = short_conv(qt, query_taps, start, 2 * BLOCK)
                row = lax.broadcasted_iota(jnp.int32, (2 * BLOCK, LANES), 0) + start
                mixed = jnp.where(row < length, query * filtered, 0.0).astype(BF16)
                mixed_ref[start : start + 2 * BLOCK, cols] = mixed
                summed = res_ref[start : start + 2 * BLOCK, cols].astype(F32) + mixed.astype(F32)
                acc[start - 128 : start - 128 + 2 * BLOCK, :] += summed * summed
        return carry

    lax.fori_loop(0, WIDE // (2 * LANES), pair, 0)

    @pl.when(step == pl.num_programs(0) - 1)
    def _():
        sum_ref[...] = jnp.sum(acc[...].T, axis=0, keepdims=True)


def main_call(group_size, stretch_lengths, queries, mixed_in, residual, short_taps, filter_rows):
    rows, width = queries.shape
    groups = width // group_size
    if len(filter_rows.shape) == 2:
        filter_spec = pl.BlockSpec(filter_rows.shape, lambda p, *_: (0, 0))
    else:
        filter_spec = pl.BlockSpec((filter_rows.shape[0], 16, STEP), lambda p, *_: (0, PACKED // 16 - 1, 0))
    block = pl.BlockSpec((rows, WIDE), lambda p, *_: (0, p))
    return pl.pallas_call(
        functools.partial(main_kernel, group_size),
        grid_spec=pltpu.PrefetchScalarGridSpec(
            num_scalar_prefetch=1,
            grid=(width // WIDE,),
            in_specs=[
                block,
                block,
                block,
                pl.BlockSpec((3, 7, WIDE), lambda p, *_: (0, 0, p)),
                filter_spec,
            ],
            out_specs=[
                block,
                pl.BlockSpec((1, rows - 128), lambda p, *_: (0, 0)),
                pl.BlockSpec((groups, WINDOW), lambda p, *_: (0, 0)),
            ],
            scratch_shapes=[
                pltpu.VMEM((2, rows + 8, LANES), F32),
                pltpu.VMEM((rows - 128, LANES), F32),
            ],
        ),
        out_shape=[
            jax.ShapeDtypeStruct((rows, width), BF16),
            jax.ShapeDtypeStruct((1, rows - 128), F32),
            jax.ShapeDtypeStruct((groups, WINDOW), F32),
        ],
        compiler_params=params(),
        cost_estimate=cost(rows * width * 2 * WINDOW * 8, rows * width * 12),
        name="conv",
    )(stretch_lengths, queries, mixed_in, residual, short_taps, filter_rows)


def head_kernel(group_size, pred_ref, len_ref, held, q_ref, k_ref, v_ref, u_ref, res_ref, taps_ref, lines_ref, kept_ref, mixed_ref, sum_ref, qs, ks, vs, acc):
    del kept_ref
    step = pl.program_id(0)
    per_lane = LANES // group_size
    device = lax.axis_index("seq")
    length = len_ref[device]
    follows = pred_ref[device] >= 0

    @pl.when(step == 0)
    def _():
        acc[...] = jnp.zeros_like(acc)

    def pair(index, carry):
        for tile in range(2):
            number = index * 2 + tile
            cols = pl.ds(pl.multiple_of(number * LANES, LANES), LANES)
            here = slice(tile * LANES, (tile + 1) * LANES)
            qt, kt, vt = qs.at[tile], ks.at[tile], vs.at[tile]
            prev = jnp.where(follows, held[index, 128:PACKED, here].astype(F32), 0.0)
            qt[0:8, :] = prev[0:8]
            kt[0:8, :] = prev[8:16]
            vt[0:8, :] = prev[16:24]
            qt[8 : OPENING + 8, :] = q_ref[:, cols].astype(F32)
            kt[8:24, :] = k_ref[:, cols].astype(F32)
            vt[8:24, :] = v_ref[:, cols].astype(F32)
            query_taps = taps_ref[0, :, cols].astype(F32)
            key = short_conv(kt, taps_ref[1, :, cols].astype(F32), 0, 16)
            value = short_conv(vt, taps_ref[2, :, cols].astype(F32), 0, 16)
            opening = (key * value).astype(BF16)
            state = held[index, 0:128, here]
            state = jnp.where(follows, state, jnp.zeros_like(state))
            pad = jnp.zeros((WINDOW - BLOCK - 128, LANES), BF16)
            extended = jnp.concatenate([pad, state, opening, u_ref[16:192, cols]])
            base = pl.multiple_of(number * per_lane, per_lane)
            matrix = toeplitz(lines_ref[pl.ds(base, per_lane), :])
            parts = []
            for first in range(0, 128, 2 * BLOCK):
                windows = [extended[low : low + WINDOW] for low in (first, first + BLOCK)]
                result = jnp.dot(matrix, jnp.concatenate(windows, axis=1), preferred_element_type=F32)
                picked = pick_groups(result, group_size)
                parts.append((first, 2 * BLOCK, jnp.concatenate([picked[:, :LANES], picked[:, LANES:]])))
            edge = OPENING - 128
            edge_matrix = jnp.concatenate([matrix[g * BLOCK : g * BLOCK + edge] for g in range(per_lane)])
            edge_result = jnp.dot(edge_matrix, extended[128 : 128 + WINDOW], preferred_element_type=F32)
            parts.append((128, edge, pick_groups(edge_result, group_size, edge)))
            for first, rows, filtered in parts:
                query = short_conv(qt, query_taps, first, rows)
                row = lax.broadcasted_iota(jnp.int32, (rows, LANES), 0) + first
                mixed = jnp.where(row < length, query * filtered, 0.0).astype(BF16)
                mixed_ref[first : first + rows, cols] = mixed
                summed = res_ref[first : first + rows, cols].astype(F32) + mixed.astype(F32)
                acc[first : first + rows, :] += summed * summed
        return carry

    lax.fori_loop(0, WIDE // STEP, pair, 0)

    @pl.when(step == pl.num_programs(0) - 1)
    def _():
        sum_ref[...] = jnp.sum(acc[...].T, axis=0, keepdims=True)


def head_call(group_size, predecessor, stretch_lengths, previous, queries, keys_in, values_in, mixed_in, residual, short_taps, lines, mixed):
    rows, width = queries.shape
    per_step = WIDE // group_size
    block = pl.BlockSpec((OPENING, WIDE), lambda p, *_: (0, p))
    small = pl.BlockSpec((16, WIDE), lambda p, *_: (0, p))
    return pl.pallas_call(
        functools.partial(head_kernel, group_size),
        grid_spec=pltpu.PrefetchScalarGridSpec(
            num_scalar_prefetch=2,
            grid=(width // WIDE,),
            in_specs=[
                pl.BlockSpec((WIDE // STEP, PACKED, STEP), lambda p, *_: (p, 0, 0)),
                block,
                small,
                small,
                pl.BlockSpec((192, WIDE), lambda p, *_: (0, p)),
                block,
                pl.BlockSpec((3, 7, WIDE), lambda p, *_: (0, 0, p)),
                pl.BlockSpec((per_step, WINDOW), lambda p, *_: (p, 0)),
                pl.BlockSpec(memory_space=pl.ANY),
            ],
            out_specs=[block, pl.BlockSpec((1, 256), lambda p, *_: (0, 0))],
            scratch_shapes=[
                pltpu.VMEM((2, OPENING + 8, LANES), F32),
                pltpu.VMEM((2, 24, LANES), F32),
                pltpu.VMEM((2, 24, LANES), F32),
                pltpu.VMEM((256, LANES), F32),
            ],
        ),
        out_shape=[
            jax.ShapeDtypeStruct((rows, width), BF16),
            jax.ShapeDtypeStruct((1, 256), F32),
        ],
        input_output_aliases={10: 0},
        compiler_params=params(),
        cost_estimate=cost(128 * width * 2 * WINDOW * 8, 128 * width * 12),
        name="head",
    )(predecessor, stretch_lengths, previous, queries, keys_in, values_in, mixed_in, residual, short_taps, lines, mixed)


def norm_kernel(channels, first_block, sums, len_ref, *refs):
    sum_refs, (mixed_ref, res_ref, gain_ref), out_ref = refs[:sums], refs[sums : sums + 3], refs[-1]
    rows = mixed_ref.shape[0]
    first = (pl.program_id(0) + first_block) * rows
    length = len_ref[lax.axis_index("seq")]
    total = sum_refs[0][...]
    for ref in sum_refs[1:]:
        total = total + ref[...]
    scale = jnp.broadcast_to(lax.rsqrt(total / channels + EPSILON), (LANES, total.shape[1])).T[:rows]
    scale = jnp.where(lax.broadcasted_iota(jnp.int32, (rows, LANES), 0) + first < length, scale, 0.0)
    for lane in range(0, mixed_ref.shape[1], LANES):
        cols = slice(lane, lane + LANES)
        gain = gain_ref[:, cols].astype(F32)
        summed = res_ref[:, cols].astype(F32) + mixed_ref[:, cols].astype(F32)
        out_ref[:, cols] = (summed * scale * gain).astype(BF16)


def norm_call(channels, opening, stretch_lengths, totals, mixed, residual, gain, normed=None):
    rows, width = mixed.shape
    size, first_block, steps, lanes = (OPENING, 0, 1, 256) if opening else (128, 1, rows // 128 - 1, 128)
    block = pl.BlockSpec((size, width), lambda p, *_: (p + first_block, 0))
    operands = [*totals, mixed, residual, gain]
    in_specs = [pl.BlockSpec((1, lanes), lambda p, *_: (0, p))] * len(totals)
    in_specs += [block, block, pl.BlockSpec((1, width), lambda p, *_: (0, 0))]
    aliases = {}
    if normed is not None:
        aliases = {len(operands) + 1: 0}
        operands.append(normed)
        in_specs.append(pl.BlockSpec(memory_space=pl.ANY))
    return pl.pallas_call(
        functools.partial(norm_kernel, channels, first_block, len(totals)),
        grid_spec=pltpu.PrefetchScalarGridSpec(
            num_scalar_prefetch=1, grid=(steps,), in_specs=in_specs, out_specs=block
        ),
        out_shape=jax.ShapeDtypeStruct((rows, width), BF16),
        input_output_aliases=aliases,
        compiler_params=params(),
        cost_estimate=cost(steps * size * width * 6, steps * size * width * 6),
        name="norm_opening" if opening else "norm",
    )(stretch_lengths, *operands)


def swap(array, axis, distance):
    size = lax.axis_size(axis)
    return lax.ppermute(array, axis, [(i, i ^ distance) for i in range(size)])


def exchange(pieces):
    return lax.all_to_all(pieces, "seq", split_axis=0, concat_axis=0, tiled=True)


def shares(squares):
    parts = lax.axis_size("mp")
    if parts != 4:
        return [lax.psum(squares, "mp")]
    return [squares] + [swap(squares, "mp", k) for k in range(1, parts)]


def body(queries, keys_in, values_in, residual, short_taps, mr_filter, norm_gain, predecessor, stretch_lengths):
    rows, width = queries.shape
    count = lax.axis_size("seq")
    channels = width * lax.axis_size("mp")
    group_size = width // mr_filter.shape[1]
    two_phase = width // STEP == count == 8 and mr_filter.shape == (16, LANES)
    gain = norm_gain.reshape(1, width)
    packed = tail_call(two_phase, queries, keys_in, values_in, short_taps, mr_filter)
    mixed_in = feature_call(keys_in, values_in, short_taps)
    if two_phase:
        received = exchange(packed)
        received, mixed_in, gain = lax.optimization_barrier((received, mixed_in, gain))
        routed, filter_rows = lax.optimization_barrier((route_call(predecessor, received), received))
        previous = exchange(routed)
    else:
        gathered = lax.all_gather(packed[None], "seq", axis=0, tiled=True)
        source = jnp.clip(predecessor[lax.axis_index("seq")], 0, count - 1)
        previous = lax.dynamic_index_in_dim(gathered, source, 0, keepdims=False)
        filter_rows = lax.all_gather(mr_filter, "seq", axis=0, tiled=True)
    mixed, squares, lines = main_call(
        group_size, stretch_lengths, queries, mixed_in, residual, short_taps, filter_rows
    )
    normed = norm_call(channels, False, stretch_lengths, shares(squares), mixed, residual, gain)
    previous, normed = lax.optimization_barrier((previous, normed))
    mixed, squares = head_call(
        group_size, predecessor, stretch_lengths, previous, queries, keys_in, values_in,
        mixed_in, residual, short_taps, lines, mixed,
    )
    normed = norm_call(channels, True, stretch_lengths, shares(squares), mixed, residual, gain, normed)
    return (mixed, normed)


def solution(mesh):
    in_specs = (
        P("seq", "mp"),
        P("seq", "mp"),
        P("seq", "mp"),
        P("seq", "mp"),
        P(None, None, "mp"),
        P("seq", "mp"),
        P("mp"),
        P(),
        P(),
    )
    out_specs = (P("seq", "mp"), P("seq", "mp"))
    return jax.shard_map(body, mesh=mesh, in_specs=in_specs, out_specs=out_specs, check_vma=False)
```

profile of v0, /device:TPU:0, one launch (start us, length us, event | category | flops | bytes accessed | tf_op | source)
XLA Modules:
  0.0 68.0 jit_solution(13746905025637098930)
XLA Ops:
  0.6 3.5 %tail.1 = bf16[8,160,256]{2,1,0:T(8,128)(2,1)} custom-call(bf16[512,2048]{1,0:T(8,128)(2,1)} %q_ref.5, bf16[512,2048]{1,0:T(8,128)(2,1)} %k_ref.5, bf16[512,2048]{1,0:T(8,128)(2,1)} %v_ref.5, bf16[512,2048]{1,0:T(8,128)(2,1)} %k_ref.5, bf16[512,2048]{1,0:T(8,128)(2,1)} %v_ref.5, bf16[3,7,2048]{2,1,0:T(8,128)(2,1)} %taps_ref.7, bf16[16,128]{1,0:T(8,128)(2,1)} %filt_ref.1), custom_call_target="tpu_custom_call" | custom-call | flops 7864320 | bytes 1572864 | tf_op jit(solution)/shard_map/tail/pallas_call | solution.py:71
  4.1 7.3 %all-to-all-start = ((bf16[8,160,256]{2,1,0:T(8,128)(2,1)}), bf16[8,160,256]{2,1,0:T(8,128)(2,1)}, u32[]{:S(2)}, u32[]{:S(2)}) async-start(bf16[8,160,256]{2,1,0:T(8,128)(2,1)} %tail.1), calls=%async_computation | async-start | bytes 1310720 | tf_op jit(solution)/shard_map/all_to_all | solution.py:429
  11.4 1.3 %reshape.7.refs_6_ = bf16[1,2048]{1,0:T(2,128)(2,1)} reshape(bf16[2048]{0:T(1024)(128)(2,1)} %param.15) | data formatting | bytes 8192 | tf_op jit(solution)/shard_map/reshape | solution.py:445
  12.7 6.9 %features.1.u_ref = bf16[512,2048]{1,0:T(8,128)(2,1)} custom-call(bf16[512,2048]{1,0:T(8,128)(2,1)} %k_ref.5, bf16[512,2048]{1,0:T(8,128)(2,1)} %v_ref.5, bf16[3,7,2048]{2,1,0:T(8,128)(2,1)} %taps_ref.7), custom_call_target="tpu_custom_call" | custom-call | flops 31457280 | bytes 6291456 | tf_op jit(solution)/shard_map/features/pallas_call | solution.py:117
  19.6 9.2 %all-to-all-done.in_ref.filt_ref = bf16[8,160,256]{2,1,0:T(8,128)(2,1)} async-done(((bf16[8,160,256]{2,1,0:T(8,128)(2,1)}), bf16[8,160,256]{2,1,0:T(8,128)(2,1)}, u32[]{:S(2)}, u32[]{:S(2)}) %all-to-all-start) | async-done | bytes 655392 | tf_op jit(solution)/shard_map/all_to_all | solution.py:429
  28.8 2.7 %route.1 = bf16[8,160,256]{2,1,0:T(8,128)(2,1)} custom-call(s32[8]{0:T(128)} %pred_ref.3, bf16[8,160,256]{2,1,0:T(8,128)(2,1)} %all-to-all-done.in_ref.filt_ref), custom_call_target="tpu_custom_call" | custom-call | bytes 1310720 | tf_op jit(solution)/shard_map/route/pallas_call | solution.py:141
  31.5 4.2 %all-to-all-start.1 = ((bf16[8,160,256]{2,1,0:T(8,128)(2,1)}), bf16[8,160,256]{2,1,0:T(8,128)(2,1)}, u32[]{:S(2)}, u32[]{:S(2)}) async-start(bf16[8,160,256]{2,1,0:T(8,128)(2,1)} %route.1), calls=%async_computation.1 | async-start | bytes 1310720 | tf_op jit(solution)/shard_map/all_to_all | solution.py:429
  35.8 9.5 %conv.1 = (bf16[512,2048]{1,0:T(8,128)(2,1)}, f32[1,384]{1,0:T(1,128)}, f32[128,256]{1,0:T(8,128)}) custom-call(s32[8]{0:T(128)} %len_ref.7, bf16[512,2048]{1,0:T(8,128)(2,1)} %q_ref.5, bf16[512,2048]{1,0:T(8,128)(2,1)} %features.1.u_ref, bf16[512,2048]{1,0:T(8,128)(2,1)} %refs_5_.3, bf16[3,7,2048]{2,1,0:T(8,128)(2,1)} %taps_ref.7, ...), custom_call_target="tpu_custom_call" | custom-call | flops 4294967296 | bytes 12582912 | tf_op jit(solution)/shard_map/conv/pallas_call | solution.py:247
  45.2 0.3 collective-permute-start.2
  45.5 1.3 %collective-permute-start.1 = (f32[1,384]{1,0:T(1,128)}, f32[1,384]{1,0:T(1,128)}, u32[]{:S(2)}, u32[]{:S(2)}) collective-permute-start(f32[1,384]{1,0:T(1,128)} %get-tuple-element.18.refs_0_), channel_id=1, source_target_pairs={{0,2},{1,3},{2,0},{3,1},{4,6},{5,7},{6,4},{7,5},{8,10},{9,11},{10,... | collective-permute-start | bytes 4616 | tf_op jit(solution)/shard_map/ppermute | solution.py:425
  46.9 0.3 collective-permute-start
  47.1 1.5 %collective-permute-done.2.refs_3_ = f32[1,384]{1,0:T(1,128)} collective-permute-done((f32[1,384]{1,0:T(1,128)}, f32[1,384]{1,0:T(1,128)}, u32[]{:S(2)}, u32[]{:S(2)}) %collective-permute-start.2) | collective-permute-done | bytes 1568 | tf_op jit(solution)/shard_map/ppermute | solution.py:425
  48.6 0.8 %collective-permute-done.1.refs_2_ = f32[1,384]{1,0:T(1,128)} collective-permute-done((f32[1,384]{1,0:T(1,128)}, f32[1,384]{1,0:T(1,128)}, u32[]{:S(2)}, u32[]{:S(2)}) %collective-permute-start.1) | collective-permute-done | bytes 1568 | tf_op jit(solution)/shard_map/ppermute | solution.py:425
  49.4 0.0 collective-permute-done.refs_1_
  49.4 4.9 %norm.1.refs_7_ = bf16[512,2048]{1,0:T(8,128)(2,1)} custom-call(s32[8]{0:T(128)} %len_ref.7, f32[1,384]{1,0:T(1,128)} %get-tuple-element.18.refs_0_, f32[1,384]{1,0:T(1,128)} %collective-permute-done.refs_1_, f32[1,384]{1,0:T(1,128)} %collective-permute-done.1.refs_2_, f32[1,384]{1,0:T(1,128)} %collective-permute-done.2.refs_3_, ...), custom_call_target="tpu_custom_call" | custom-call | flops 4718592 | bytes 4718592 | tf_op jit(solution)/shard_map/norm/pallas_call | solution.py:410
  54.3 0.0 all-to-all-done.1.held
  54.3 6.4 %head.1 = (bf16[512,2048]{1,0:T(8,128)(2,1)}, f32[1,256]{1,0:T(1,128)}) custom-call(s32[8]{0:T(128)} %pred_ref.3, s32[8]{0:T(128)} %len_ref.7, bf16[8,160,256]{2,1,0:T(8,128)(2,1)} %all-to-all-done.1.held, bf16[512,2048]{1,0:T(8,128)(2,1)} %q_ref.5, bf16[512,2048]{1,0:T(8,128)(2,1)} %k_ref.5, ...), custom_call_target="tpu_custom_call", output_to_operand_aliasing={{0}: (10, {})} | custom-call | flops 1073741824 | bytes 3145728 | tf_op jit(solution)/shard_map/head/pallas_call | solution.py:346
  60.7 0.4 collective-permute-start.5
  61.1 1.7 %collective-permute-start.4 = (f32[1,256]{1,0:T(1,128)}, f32[1,256]{1,0:T(1,128)}, u32[]{:S(2)}, u32[]{:S(2)}) collective-permute-start(f32[1,256]{1,0:T(1,128)} %get-tuple-element.24.refs_0_), channel_id=1, source_target_pairs={{0,2},{1,3},{2,0},{3,1},{4,6},{5,7},{6,4},{7,5},{8,10},{9,11},{10,... | collective-permute-start | bytes 3080 | tf_op jit(solution)/shard_map/ppermute | solution.py:425
  62.9 0.0 collective-permute-start.3
  62.9 1.0 %collective-permute-done.5.refs_3_ = f32[1,256]{1,0:T(1,128)} collective-permute-done((f32[1,256]{1,0:T(1,128)}, f32[1,256]{1,0:T(1,128)}, u32[]{:S(2)}, u32[]{:S(2)}) %collective-permute-start.5) | collective-permute-done | bytes 1056 | tf_op jit(solution)/shard_map/ppermute | solution.py:425
  63.9 1.1 %collective-permute-done.4.refs_2_ = f32[1,256]{1,0:T(1,128)} collective-permute-done((f32[1,256]{1,0:T(1,128)}, f32[1,256]{1,0:T(1,128)}, u32[]{:S(2)}, u32[]{:S(2)}) %collective-permute-start.4) | collective-permute-done | bytes 1056 | tf_op jit(solution)/shard_map/ppermute | solution.py:425
  65.0 0.0 collective-permute-done.3.refs_1_
  65.0 3.0 %norm_opening.1 = bf16[512,2048]{1,0:T(8,128)(2,1)} custom-call(s32[8]{0:T(128)} %len_ref.7, f32[1,256]{1,0:T(1,128)} %get-tuple-element.24.refs_0_, f32[1,256]{1,0:T(1,128)} %collective-permute-done.3.refs_1_, f32[1,256]{1,0:T(1,128)} %collective-permute-done.4.refs_2_, f32[1,256]{1,0:T(1,128)} %collective-permute-done.5.refs_3_, ...), custom_call_target="tpu_custom_call", output_to_operand_aliasing={{}: (8, {})} | custom-call | flops 1769472 | bytes 1769472 | tf_op jit(solution)/shard_map/norm_opening/pallas_call | solution.py:410
Async XLA Ops:
  4.1 24.7 %all-to-all-start = ((bf16[8,160,256]{2,1,0:T(8,128)(2,1)}), bf16[8,160,256]{2,1,0:T(8,128)(2,1)}, u32[]{:S(2)}, u32[]{:S(2)}) async-start(bf16[8,160,256]{2,1,0:T(8,128)(2,1)} %tail.1), calls=%async_computation | async-start | bytes 1310720 | tf_op jit(solution)/shard_map/all_to_all | solution.py:429
  31.5 22.8 %all-to-all-start.1 = ((bf16[8,160,256]{2,1,0:T(8,128)(2,1)}), bf16[8,160,256]{2,1,0:T(8,128)(2,1)}, u32[]{:S(2)}, u32[]{:S(2)}) async-start(bf16[8,160,256]{2,1,0:T(8,128)(2,1)} %route.1), calls=%async_computation.1 | async-start | bytes 1310720 | tf_op jit(solution)/shard_map/all_to_all | solution.py:429
  45.2 3.4 %collective-permute-start.2 = (f32[1,384]{1,0:T(1,128)}, f32[1,384]{1,0:T(1,128)}, u32[]{:S(2)}, u32[]{:S(2)}) collective-permute-start(f32[1,384]{1,0:T(1,128)} %get-tuple-element.18.refs_0_), channel_id=1, source_target_pairs={{0,3},{1,2},{2,1},{3,0},{4,7},{5,6},{6,5},{7,4},{8,11},{9,10},{10,... | collective-permute-start | bytes 4616 | tf_op jit(solution)/shard_map/ppermute | solution.py:425
  45.5 3.9 %collective-permute-start.1 = (f32[1,384]{1,0:T(1,128)}, f32[1,384]{1,0:T(1,128)}, u32[]{:S(2)}, u32[]{:S(2)}) collective-permute-start(f32[1,384]{1,0:T(1,128)} %get-tuple-element.18.refs_0_), channel_id=1, source_target_pairs={{0,2},{1,3},{2,0},{3,1},{4,6},{5,7},{6,4},{7,5},{8,10},{9,11},{10,... | collective-permute-start | bytes 4616 | tf_op jit(solution)/shard_map/ppermute | solution.py:425
  46.9 2.6 %collective-permute-start = (f32[1,384]{1,0:T(1,128)}, f32[1,384]{1,0:T(1,128)}, u32[]{:S(2)}, u32[]{:S(2)}) collective-permute-start(f32[1,384]{1,0:T(1,128)} %get-tuple-element.18.refs_0_), channel_id=1, source_target_pairs={{0,1},{1,0},{2,3},{3,2},{4,5},{5,4},{6,7},{7,6},{8,9},{9,8},{10,11... | collective-permute-start | bytes 4616 | tf_op jit(solution)/shard_map/ppermute | solution.py:425
  60.7 3.2 %collective-permute-start.5 = (f32[1,256]{1,0:T(1,128)}, f32[1,256]{1,0:T(1,128)}, u32[]{:S(2)}, u32[]{:S(2)}) collective-permute-start(f32[1,256]{1,0:T(1,128)} %get-tuple-element.24.refs_0_), channel_id=1, source_target_pairs={{0,3},{1,2},{2,1},{3,0},{4,7},{5,6},{6,5},{7,4},{8,11},{9,10},{10,... | collective-permute-start | bytes 3080 | tf_op jit(solution)/shard_map/ppermute | solution.py:425
  61.1 3.9 %collective-permute-start.4 = (f32[1,256]{1,0:T(1,128)}, f32[1,256]{1,0:T(1,128)}, u32[]{:S(2)}, u32[]{:S(2)}) collective-permute-start(f32[1,256]{1,0:T(1,128)} %get-tuple-element.24.refs_0_), channel_id=1, source_target_pairs={{0,2},{1,3},{2,0},{3,1},{4,6},{5,7},{6,4},{7,5},{8,10},{9,11},{10,... | collective-permute-start | bytes 3080 | tf_op jit(solution)/shard_map/ppermute | solution.py:425
  62.9 2.1 %collective-permute-start.3 = (f32[1,256]{1,0:T(1,128)}, f32[1,256]{1,0:T(1,128)}, u32[]{:S(2)}, u32[]{:S(2)}) collective-permute-start(f32[1,256]{1,0:T(1,128)} %get-tuple-element.24.refs_0_), channel_id=1, source_target_pairs={{0,1},{1,0},{2,3},{3,2},{4,5},{5,4},{6,7},{7,6},{8,9},{9,8},{10,11... | collective-permute-start | bytes 3080 | tf_op jit(solution)/shard_map/ppermute | solution.py:425
where the time goes:
time: 68.7 us; the launch traced here: 68 us
  Pallas kernels  36.9 us (54%)
  starting transfers between devices  15.5 us (23%)
  waiting for transfers between devices  13.6 us (20%)
  local copies, waits for them, and re-layouts  1.28 us (2%)
    all_to_all x2, starting transfers between devices, exchange(): lax.all_to_all(pieces, 'seq', split_axis=0, concat_axis=0, tiled=True)  11.5 us
    pallas_call x1, Pallas kernels, main_call(): pl.pallas_call(functools.partial(main_kernel, group_size), grid_spec=pltp...  9.46 us
    all_to_all x2, waiting for transfers between devices, exchange(): lax.all_to_all(pieces, 'seq', split_axis=0, concat_axis=0, tiled=True)  9.19 us
    pallas_call x2, Pallas kernels, norm_call(): pl.pallas_call(functools.partial(norm_kernel, channels, first_block, len(...  7.89 us
    pallas_call x1, Pallas kernels, feature_call(): pl.pallas_call(feature_kernel, grid=(width // WIDE,), in_specs=[block, bl...  6.92 us
    pallas_call x1, Pallas kernels, head_call(): pl.pallas_call(functools.partial(head_kernel, group_size), grid_spec=pltp...  6.41 us
    ppermute x6, waiting for transfers between devices, swap(): return lax.ppermute(array, axis, [(i, i ^ distance) for i in range(size)])  4.42 us
    ppermute x6, starting transfers between devices, swap(): return lax.ppermute(array, axis, [(i, i ^ distance) for i in range(size)])  4.05 us
  transfers between devices with their start and end apart: 8, of which 5 were waited for; matrix products, arithmetic and copies ran while one was open for 2% of the time, Pallas kernels for 31%

commit v1 on v0

--- a/solution.py
+++ b/solution.py
@@ -89,61 +89,61 @@
     )(queries, keys_in, values_in, keys_in, values_in, short_taps, mr_filter)
 
 
-def feature_kernel(k_ref, v_ref, taps_ref, out_ref, ks, vs):
+def feature_kernel(q_ref, k_ref, v_ref, taps_ref, out_ref, opening_ref, later_ref, qs, ks, vs):
     rows = k_ref.shape[0]
 
     def pair(index, carry):
         for tile in range(2):
             cols = pl.ds(pl.multiple_of(index * 2 * LANES + tile * LANES, LANES), LANES)
-            kt, vt = ks.at[tile], vs.at[tile]
-            kt[0:8, :] = jnp.zeros((8, LANES), F32)
-            vt[0:8, :] = jnp.zeros((8, LANES), F32)
-            kt[8 : rows + 8, :] = k_ref[:, cols].astype(F32)
-            vt[8 : rows + 8, :] = v_ref[:, cols].astype(F32)
-            key_taps = taps_ref[1, :, cols].astype(F32)
-            value_taps = taps_ref[2, :, cols].astype(F32)
+            scratches = (qs.at[tile], ks.at[tile], vs.at[tile])
+            taps = [taps_ref[i, :, cols].astype(F32) for i in range(3)]
+            for scratch, ref in zip(scratches, (q_ref, k_ref, v_ref)):
+                scratch[0:8, :] = jnp.zeros((8, LANES), F32)
+                scratch[8 : rows + 8, :] = ref[:, cols].astype(F32)
             for row in range(0, rows, 64):
-                key = short_conv(kt, key_taps, row, 64)
-                value = short_conv(vt, value_taps, row, 64)
+                query, key, value = [short_conv(x, t, row, 64) for x, t in zip(scratches, taps)]
                 out_ref[row : row + 64, cols] = (key * value).astype(BF16)
+                if row < OPENING:
+                    count = min(64, OPENING - row)
+                    opening_ref[row : row + count, cols] = query[:count]
+                if row >= 128:
+                    later_ref[row - 128 : row - 64, cols] = query
         return carry
 
     lax.fori_loop(0, k_ref.shape[1] // (2 * LANES), pair, 0)
 
 
-def feature_call(keys_in, values_in, short_taps):
+def feature_call(queries, keys_in, values_in, short_taps):
     rows, width = keys_in.shape
-    block = pl.BlockSpec((rows, WIDE), lambda p: (0, p))
+    heights = (rows, OPENING, rows - 128)
+    blocks = [pl.BlockSpec((height, WIDE), lambda p: (0, p)) for height in heights]
+    scratch = pltpu.VMEM((2, rows + 8, LANES), F32)
     return pl.pallas_call(
         feature_kernel,
         grid=(width // WIDE,),
-        in_specs=[block, block, pl.BlockSpec((3, 7, WIDE), lambda p: (0, 0, p))],
-        out_specs=block,
-        out_shape=jax.ShapeDtypeStruct((rows, width), BF16),
-        scratch_shapes=[pltpu.VMEM((2, rows + 8, LANES), F32), pltpu.VMEM((2, rows + 8, LANES), F32)],
-        compiler_params=params(),
-        cost_estimate=cost(rows * width * 30, rows * width * 6),
+        in_specs=[blocks[0]] * 3 + [pl.BlockSpec((3, 7, WIDE), lambda p: (0, 0, p))],
+        out_specs=blocks,
+        out_shape=[
+            jax.ShapeDtypeStruct((height, width), kind) for height, kind in zip(heights, (BF16, F32, F32))
+        ],
+        scratch_shapes=[scratch] * 3,
+        compiler_params=params(),
+        cost_estimate=cost(rows * width * 45, rows * width * 13),
         name="features",
-    )(keys_in, values_in, short_taps)
-
-
-def route_kernel(pred_ref, in_ref, out_ref, sems):
-    copies = []
+    )(queries, keys_in, values_in, short_taps)
+
+
+def route_kernel(pred_ref, in_ref, out_ref):
     for j in range(in_ref.shape[0]):
-        source = jnp.maximum(pred_ref[j], 0)
-        copies.append(pltpu.make_async_copy(in_ref.at[source], out_ref.at[j], sems.at[j]))
-        copies[-1].start()
-    for copy in copies:
-        copy.wait()
+        out_ref[j] = in_ref[jnp.maximum(pred_ref[j], 0)]
 
 
 def route_call(predecessor, received):
     return pl.pallas_call(
         route_kernel,
-        in_specs=[pl.BlockSpec(memory_space=pltpu.SMEM), pl.BlockSpec(memory_space=pl.ANY)],
+        in_specs=[pl.BlockSpec(memory_space=pltpu.SMEM), pl.BlockSpec(memory_space=pltpu.VMEM)],
         out_specs=pl.BlockSpec(memory_space=pltpu.VMEM),
         out_shape=jax.ShapeDtypeStruct(received.shape, BF16),
-        scratch_shapes=[pltpu.SemaphoreType.DMA((received.shape[0],))],
         compiler_params=params(),
         cost_estimate=cost(0, received.size * 4),
         name="route",
@@ -185,9 +185,9 @@
     return picked
 
 
-def main_kernel(group_size, len_ref, q_ref, u_ref, res_ref, taps_ref, filt_ref, mixed_ref, sum_ref, lines_ref, qs, acc):
+def main_kernel(group_size, len_ref, query_ref, u_ref, res_ref, filt_ref, mixed_ref, sum_ref, lines_ref, acc):
     step = pl.program_id(0)
-    rows = q_ref.shape[0]
+    rows = u_ref.shape[0]
     per_lane = LANES // group_size
     length = len_ref[lax.axis_index("seq")]
 
@@ -202,10 +202,6 @@
         for tile in range(2):
             number = index * 2 + tile
             cols = pl.ds(pl.multiple_of(number * LANES, LANES), LANES)
-            qt = qs.at[tile]
-            qt[0:8, :] = jnp.zeros((8, LANES), F32)
-            qt[8 : rows + 8, :] = q_ref[:, cols].astype(F32)
-            query_taps = taps_ref[0, :, cols].astype(F32)
             base = pl.multiple_of((step * (WIDE // LANES) + number) * per_lane, per_lane)
             matrix = toeplitz(lines_ref[pl.ds(base, per_lane), :])
             for start in range(128, rows, 2 * BLOCK):
@@ -221,7 +217,7 @@
                 result = jnp.dot(matrix, jnp.concatenate(windows, axis=1), preferred_element_type=F32)
                 picked = pick_groups(result, group_size)
                 filtered = jnp.concatenate([picked[:, :LANES], picked[:, LANES:]])
-                query = short_conv(qt, query_taps, start, 2 * BLOCK)
+                query = query_ref[start - 128 : start - 128 + 2 * BLOCK, cols]
                 row = lax.broadcasted_iota(jnp.int32, (2 * BLOCK, LANES), 0) + start
                 mixed = jnp.where(row < length, query * filtered, 0.0).astype(BF16)
                 mixed_ref[start : start + 2 * BLOCK, cols] = mixed
@@ -236,8 +232,8 @@
         sum_ref[...] = jnp.sum(acc[...].T, axis=0, keepdims=True)
 
 
-def main_call(group_size, stretch_lengths, queries, mixed_in, residual, short_taps, filter_rows):
-    rows, width = queries.shape
+def main_call(group_size, stretch_lengths, query_later, mixed_in, residual, filter_rows):
+    rows, width = residual.shape
     groups = width // group_size
     if len(filter_rows.shape) == 2:
         filter_spec = pl.BlockSpec(filter_rows.shape, lambda p, *_: (0, 0))
@@ -250,10 +246,9 @@
             num_scalar_prefetch=1,
             grid=(width // WIDE,),
             in_specs=[
+                pl.BlockSpec((rows - 128, WIDE), lambda p, *_: (0, p)),
                 block,
                 block,
-                block,
-                pl.BlockSpec((3, 7, WIDE), lambda p, *_: (0, 0, p)),
                 filter_spec,
             ],
             out_specs=[
@@ -262,7 +257,6 @@
                 pl.BlockSpec((groups, WINDOW), lambda p, *_: (0, 0)),
             ],
             scratch_shapes=[
-                pltpu.VMEM((2, rows + 8, LANES), F32),
                 pltpu.VMEM((rows - 128, LANES), F32),
             ],
         ),
@@ -274,10 +268,10 @@
         compiler_params=params(),
         cost_estimate=cost(rows * width * 2 * WINDOW * 8, rows * width * 12),
         name="conv",
-    )(stretch_lengths, queries, mixed_in, residual, short_taps, filter_rows)
-
-
-def head_kernel(group_size, pred_ref, len_ref, held, q_ref, k_ref, v_ref, u_ref, res_ref, taps_ref, lines_ref, kept_ref, mixed_ref, sum_ref, qs, ks, vs, acc):
+    )(stretch_lengths, query_later, mixed_in, residual, filter_rows)
+
+
+def head_kernel(group_size, pred_ref, len_ref, held, query_ref, q_ref, k_ref, v_ref, u_ref, res_ref, taps_ref, lines_ref, kept_ref, mixed_ref, sum_ref, qs, ks, vs, acc):
     del kept_ref
     step = pl.program_id(0)
     per_lane = LANES // group_size
@@ -299,10 +293,10 @@
             qt[0:8, :] = prev[0:8]
             kt[0:8, :] = prev[8:16]
             vt[0:8, :] = prev[16:24]
-            qt[8 : OPENING + 8, :] = q_ref[:, cols].astype(F32)
+            qt[8:24, :] = q_ref[:, cols].astype(F32)
             kt[8:24, :] = k_ref[:, cols].astype(F32)
             vt[8:24, :] = v_ref[:, cols].astype(F32)
-            query_taps = taps_ref[0, :, cols].astype(F32)
+            first_query = short_conv(qt, taps_ref[0, :, cols].astype(F32), 0, 16)
             key = short_conv(kt, taps_ref[1, :, cols].astype(F32), 0, 16)
             value = short_conv(vt, taps_ref[2, :, cols].astype(F32), 0, 16)
             opening = (key * value).astype(BF16)
@@ -323,7 +317,9 @@
             edge_result = jnp.dot(edge_matrix, extended[128 : 128 + WINDOW], preferred_element_type=F32)
             parts.append((128, edge, pick_groups(edge_result, group_size, edge)))
             for first, rows, filtered in parts:
-                query = short_conv(qt, query_taps, first, rows)
+                query = query_ref[first : first + rows, cols]
+                if first == 0:
+                    query = jnp.concatenate([first_query, query[16:]])
                 row = lax.broadcasted_iota(jnp.int32, (rows, LANES), 0) + first
                 mixed = jnp.where(row < length, query * filtered, 0.0).astype(BF16)
                 mixed_ref[first : first + rows, cols] = mixed
@@ -338,7 +334,7 @@
         sum_ref[...] = jnp.sum(acc[...].T, axis=0, keepdims=True)
 
 
-def head_call(group_size, predecessor, stretch_lengths, previous, queries, keys_in, values_in, mixed_in, residual, short_taps, lines, mixed):
+def head_call(group_size, predecessor, stretch_lengths, previous, query_opening, queries, keys_in, values_in, mixed_in, residual, short_taps, lines, mixed):
     rows, width = queries.shape
     per_step = WIDE // group_size
     block = pl.BlockSpec((OPENING, WIDE), lambda p, *_: (0, p))
@@ -351,6 +347,7 @@
             in_specs=[
                 pl.BlockSpec((WIDE // STEP, PACKED, STEP), lambda p, *_: (p, 0, 0)),
                 block,
+                small,
                 small,
                 small,
                 pl.BlockSpec((192, WIDE), lambda p, *_: (0, p)),
@@ -361,7 +358,7 @@
             ],
             out_specs=[block, pl.BlockSpec((1, 256), lambda p, *_: (0, 0))],
             scratch_shapes=[
-                pltpu.VMEM((2, OPENING + 8, LANES), F32),
+                pltpu.VMEM((2, 24, LANES), F32),
                 pltpu.VMEM((2, 24, LANES), F32),
                 pltpu.VMEM((2, 24, LANES), F32),
                 pltpu.VMEM((256, LANES), F32),
@@ -371,11 +368,11 @@
             jax.ShapeDtypeStruct((rows, width), BF16),
             jax.ShapeDtypeStruct((1, 256), F32),
         ],
-        input_output_aliases={10: 0},
+        input_output_aliases={11: 0},
         compiler_params=params(),
         cost_estimate=cost(128 * width * 2 * WINDOW * 8, 128 * width * 12),
         name="head",
-    )(predecessor, stretch_lengths, previous, queries, keys_in, values_in, mixed_in, residual, short_taps, lines, mixed)
+    )(predecessor, stretch_lengths, previous, query_opening, queries, keys_in, values_in, mixed_in, residual, short_taps, lines, mixed)
 
 
 def norm_kernel(channels, first_block, sums, len_ref, *refs):
@@ -444,7 +441,7 @@
     two_phase = width // STEP == count == 8 and mr_filter.shape == (16, LANES)
     gain = norm_gain.reshape(1, width)
     packed = tail_call(two_phase, queries, keys_in, values_in, short_taps, mr_filter)
-    mixed_in = feature_call(keys_in, values_in, short_taps)
+    mixed_in, query_opening, query_later = feature_call(queries, keys_in, values_in, short_taps)
     if two_phase:
         received = exchange(packed)
         received, mixed_in, gain = lax.optimization_barrier((received, mixed_in, gain))
@@ -456,12 +453,12 @@
         previous = lax.dynamic_index_in_dim(gathered, source, 0, keepdims=False)
         filter_rows = lax.all_gather(mr_filter, "seq", axis=0, tiled=True)
     mixed, squares, lines = main_call(
-        group_size, stretch_lengths, queries, mixed_in, residual, short_taps, filter_rows
+        group_size, stretch_lengths, query_later, mixed_in, residual, filter_rows
     )
     normed = norm_call(channels, False, stretch_lengths, shares(squares), mixed, residual, gain)
     previous, normed = lax.optimization_barrier((previous, normed))
     mixed, squares = head_call(
-        group_size, predecessor, stretch_lengths, previous, queries, keys_in, values_in,
+        group_size, predecessor, stretch_lengths, previous, query_opening, queries, keys_in, values_in,
         mixed_in, residual, short_taps, lines, mixed,
     )
     normed = norm_call(channels, True, stretch_lengths, shares(squares), mixed, residual, gain, normed)

time: 68.7 us -> 67.6 us (0.984)
  waiting for transfers between devices: 13.6 us -> 10.8 us
  Pallas kernels: 36.9 us -> 38.5 us
    pallas_call x1, Pallas kernels: 6.92 us -> 9.69 us  [feature_call(): pl.pallas_call(feature_kernel, grid=(width // WIDE,), in_specs=[blocks[0]...]
    all_to_all x2, waiting for transfers between devices: 9.19 us -> 6.43 us  [exchange(): lax.all_to_all(pieces, 'seq', split_axis=0, concat_axis=0, tiled=True)]
    pallas_call x1, Pallas kernels: 2.74 us -> 1.96 us  [route_call(): pl.pallas_call(route_kernel, in_specs=[pl.BlockSpec(memory_space=pltpu.SM...]
  transfers between devices with their start and end apart: 8 -> 8, of which waited for: 5 -> 5; matrix products, arithmetic and copies ran while one was open for 2% -> 2% of each run, Pallas kernels for 31% -> 35%
where the time goes in v1:
time: 67.6 us; the launch traced here: 66.9 us
  Pallas kernels  38.5 us (57%)
  starting transfers between devices  15.7 us (23%)
  waiting for transfers between devices  10.8 us (16%)
  local copies, waits for them, and re-layouts  1.28 us (2%)
    all_to_all x2, starting transfers between devices, exchange(): lax.all_to_all(pieces, 'seq', split_axis=0, concat_axis=0, tiled=True)  11.5 us
    pallas_call x1, Pallas kernels, feature_call(): pl.pallas_call(feature_kernel, grid=(width // WIDE,), in_specs=[blocks[0]...  9.69 us
    pallas_call x1, Pallas kernels, main_call(): pl.pallas_call(functools.partial(main_kernel, group_size), grid_spec=pltp...  8.98 us
    pallas_call x2, Pallas kernels, norm_call(): pl.pallas_call(functools.partial(norm_kernel, channels, first_block, len(...  7.89 us
    pallas_call x1, Pallas kernels, head_call(): pl.pallas_call(functools.partial(head_kernel, group_size), grid_spec=pltp...  6.49 us
    all_to_all x2, waiting for transfers between devices, exchange(): lax.all_to_all(pieces, 'seq', split_axis=0, concat_axis=0, tiled=True)  6.43 us
    ppermute x6, waiting for transfers between devices, swap(): return lax.ppermute(array, axis, [(i, i ^ distance) for i in range(size)])  4.36 us
    ppermute x6, starting transfers between devices, swap(): return lax.ppermute(array, axis, [(i, i ^ distance) for i in range(size)])  4.2 us
  transfers between devices with their start and end apart: 8, of which 5 were waited for; matrix products, arithmetic and copies ran while one was open for 2% of the time, Pallas kernels for 35%

profile of v1, /device:TPU:0, one launch (start us, length us, event | category | flops | bytes accessed | tf_op | source)
XLA Modules:
  0.0 66.9 jit_solution(5911725559783824126)
XLA Ops:
  0.6 3.5 %tail.1 = bf16[8,160,256]{2,1,0:T(8,128)(2,1)} custom-call(bf16[512,2048]{1,0:T(8,128)(2,1)} %q_ref.5, bf16[512,2048]{1,0:T(8,128)(2,1)} %k_ref.5, bf16[512,2048]{1,0:T(8,128)(2,1)} %v_ref.5, bf16[512,2048]{1,0:T(8,128)(2,1)} %k_ref.5, bf16[512,2048]{1,0:T(8,128)(2,1)} %v_ref.5, bf16[3,7,2048]{2,1,0:T(8,128)(2,1)} %taps_ref.5, bf16[16,128]{1,0:T(8,128)(2,1)} %filt_ref.1), custom_call_target="tpu_custom_call" | custom-call | flops 7864320 | bytes 1572864 | tf_op jit(solution)/shard_map/tail/pallas_call | solution.py:71
  4.1 7.3 %all-to-all-start = ((bf16[8,160,256]{2,1,0:T(8,128)(2,1)}), bf16[8,160,256]{2,1,0:T(8,128)(2,1)}, u32[]{:S(2)}, u32[]{:S(2)}) async-start(bf16[8,160,256]{2,1,0:T(8,128)(2,1)} %tail.1), calls=%async_computation | async-start | bytes 1310720 | tf_op jit(solution)/shard_map/all_to_all | solution.py:426
  11.4 1.3 %reshape.7.refs_6_ = bf16[1,2048]{1,0:T(2,128)(2,1)} reshape(bf16[2048]{0:T(1024)(128)(2,1)} %param.15) | data formatting | bytes 8192 | tf_op jit(solution)/shard_map/reshape | solution.py:442
  12.7 9.7 %features.1 = (bf16[512,2048]{1,0:T(8,128)(2,1)}, f32[144,2048]{1,0:T(8,128)}, f32[384,2048]{1,0:T(8,128)}) custom-call(bf16[512,2048]{1,0:T(8,128)(2,1)} %q_ref.5, bf16[512,2048]{1,0:T(8,128)(2,1)} %k_ref.5, bf16[512,2048]{1,0:T(8,128)(2,1)} %v_ref.5, bf16[3,7,2048]{2,1,0:T(8,128)(2,1)} %taps_ref.5), custom_call_target="tpu_custom_call" | custom-call | flops 47185920 | bytes 13631488 | tf_op jit(solution)/shard_map/features/pallas_call | solution.py:121
  22.4 6.4 %all-to-all-done.in_ref.filt_ref = bf16[8,160,256]{2,1,0:T(8,128)(2,1)} async-done(((bf16[8,160,256]{2,1,0:T(8,128)(2,1)}), bf16[8,160,256]{2,1,0:T(8,128)(2,1)}, u32[]{:S(2)}, u32[]{:S(2)}) %all-to-all-start) | async-done | bytes 655392 | tf_op jit(solution)/shard_map/all_to_all | solution.py:426
  28.8 2.0 %route.1 = bf16[8,160,256]{2,1,0:T(8,128)(2,1)} custom-call(s32[8]{0:T(128)} %pred_ref.3, bf16[8,160,256]{2,1,0:T(8,128)(2,1)} %all-to-all-done.in_ref.filt_ref), custom_call_target="tpu_custom_call" | custom-call | bytes 1310720 | tf_op jit(solution)/shard_map/route/pallas_call | solution.py:142
  30.8 4.2 %all-to-all-start.1 = ((bf16[8,160,256]{2,1,0:T(8,128)(2,1)}), bf16[8,160,256]{2,1,0:T(8,128)(2,1)}, u32[]{:S(2)}, u32[]{:S(2)}) async-start(bf16[8,160,256]{2,1,0:T(8,128)(2,1)} %route.1), calls=%async_computation.1 | async-start | bytes 1310720 | tf_op jit(solution)/shard_map/all_to_all | solution.py:426
  35.0 9.0 %conv.1 = (bf16[512,2048]{1,0:T(8,128)(2,1)}, f32[1,384]{1,0:T(1,128)}, f32[128,256]{1,0:T(8,128)}) custom-call(s32[8]{0:T(128)} %len_ref.7, f32[384,2048]{1,0:T(8,128)} %get-tuple-element.20.query_ref, bf16[512,2048]{1,0:T(8,128)(2,1)} %get-tuple-element.21.u_ref, bf16[512,2048]{1,0:T(8,128)(2,1)} %refs_5_.3, bf16[8,160,256]{2,1,0:T(8,128)(2,1)} %all-to-all-done.in_ref.filt_ref), custom_call_target="tpu_custom_call" | custom-call | flops 4294967296 | bytes 12582912 | tf_op jit(solution)/shard_map/conv/pallas_call | solution.py:243
  43.9 0.3 collective-permute-start.2
  44.2 1.3 %collective-permute-start.1 = (f32[1,384]{1,0:T(1,128)}, f32[1,384]{1,0:T(1,128)}, u32[]{:S(2)}, u32[]{:S(2)}) collective-permute-start(f32[1,384]{1,0:T(1,128)} %get-tuple-element.23.refs_0_), channel_id=1, source_target_pairs={{0,2},{1,3},{2,0},{3,1},{4,6},{5,7},{6,4},{7,5},{8,10},{9,11},{10,... | collective-permute-start | bytes 4616 | tf_op jit(solution)/shard_map/ppermute | solution.py:422
  45.5 0.3 collective-permute-start
  45.8 1.3 %collective-permute-done.2.refs_3_ = f32[1,384]{1,0:T(1,128)} collective-permute-done((f32[1,384]{1,0:T(1,128)}, f32[1,384]{1,0:T(1,128)}, u32[]{:S(2)}, u32[]{:S(2)}) %collective-permute-start.2) | collective-permute-done | bytes 1568 | tf_op jit(solution)/shard_map/ppermute | solution.py:422
  47.1 0.8 %collective-permute-done.1.refs_2_ = f32[1,384]{1,0:T(1,128)} collective-permute-done((f32[1,384]{1,0:T(1,128)}, f32[1,384]{1,0:T(1,128)}, u32[]{:S(2)}, u32[]{:S(2)}) %collective-permute-start.1) | collective-permute-done | bytes 1568 | tf_op jit(solution)/shard_map/ppermute | solution.py:422
  47.9 0.0 collective-permute-done.refs_1_
  48.0 4.9 %norm.1.refs_7_ = bf16[512,2048]{1,0:T(8,128)(2,1)} custom-call(s32[8]{0:T(128)} %len_ref.7, f32[1,384]{1,0:T(1,128)} %get-tuple-element.23.refs_0_, f32[1,384]{1,0:T(1,128)} %collective-permute-done.refs_1_, f32[1,384]{1,0:T(1,128)} %collective-permute-done.1.refs_2_, f32[1,384]{1,0:T(1,128)} %collective-permute-done.2.refs_3_, ...), custom_call_target="tpu_custom_call" | custom-call | flops 4718592 | bytes 4718592 | tf_op jit(solution)/shard_map/norm/pallas_call | solution.py:407
  52.8 0.0 all-to-all-done.1.held
  52.9 6.5 %head.1 = (bf16[512,2048]{1,0:T(8,128)(2,1)}, f32[1,256]{1,0:T(1,128)}) custom-call(s32[8]{0:T(128)} %pred_ref.3, s32[8]{0:T(128)} %len_ref.7, bf16[8,160,256]{2,1,0:T(8,128)(2,1)} %all-to-all-done.1.held, f32[144,2048]{1,0:T(8,128)} %get-tuple-element.27.query_ref, bf16[512,2048]{1,0:T(8,128)(2,1)} %q_ref.5, ...), custom_call_target="tpu_custom_call", output_to_operand_aliasing={{0}: (11, {})} | custom-call | flops 1073741824 | bytes 3145728 | tf_op jit(solution)/shard_map/head/pallas_call | solution.py:342
  59.3 0.8 %collective-permute-start.5 = (f32[1,256]{1,0:T(1,128)}, f32[1,256]{1,0:T(1,128)}, u32[]{:S(2)}, u32[]{:S(2)}) collective-permute-start(f32[1,256]{1,0:T(1,128)} %get-tuple-element.30.refs_0_), channel_id=1, source_target_pairs={{0,3},{1,2},{2,1},{3,0},{4,7},{5,6},{6,5},{7,4},{8,11},{9,10},{10,... | collective-permute-start | bytes 3080 | tf_op jit(solution)/shard_map/ppermute | solution.py:422
  60.2 1.5 %collective-permute-start.4 = (f32[1,256]{1,0:T(1,128)}, f32[1,256]{1,0:T(1,128)}, u32[]{:S(2)}, u32[]{:S(2)}) collective-permute-start(f32[1,256]{1,0:T(1,128)} %get-tuple-element.30.refs_0_), channel_id=1, source_target_pairs={{0,2},{1,3},{2,0},{3,1},{4,6},{5,7},{6,4},{7,5},{8,10},{9,11},{10,... | collective-permute-start | bytes 3080 | tf_op jit(solution)/shard_map/ppermute | solution.py:422
  61.7 0.0 collective-permute-start.3
  61.7 0.9 %collective-permute-done.5.refs_3_ = f32[1,256]{1,0:T(1,128)} collective-permute-done((f32[1,256]{1,0:T(1,128)}, f32[1,256]{1,0:T(1,128)}, u32[]{:S(2)}, u32[]{:S(2)}) %collective-permute-start.5) | collective-permute-done | bytes 1056 | tf_op jit(solution)/shard_map/ppermute | solution.py:422
  62.5 1.4 %collective-permute-done.4.refs_2_ = f32[1,256]{1,0:T(1,128)} collective-permute-done((f32[1,256]{1,0:T(1,128)}, f32[1,256]{1,0:T(1,128)}, u32[]{:S(2)}, u32[]{:S(2)}) %collective-permute-start.4) | collective-permute-done | bytes 1056 | tf_op jit(solution)/shard_map/ppermute | solution.py:422
  63.9 0.0 collective-permute-done.3.refs_1_
  63.9 3.0 %norm_opening.1 = bf16[512,2048]{1,0:T(8,128)(2,1)} custom-call(s32[8]{0:T(128)} %len_ref.7, f32[1,256]{1,0:T(1,128)} %get-tuple-element.30.refs_0_, f32[1,256]{1,0:T(1,128)} %collective-permute-done.3.refs_1_, f32[1,256]{1,0:T(1,128)} %collective-permute-done.4.refs_2_, f32[1,256]{1,0:T(1,128)} %collective-permute-done.5.refs_3_, ...), custom_call_target="tpu_custom_call", output_to_operand_aliasing={{}: (8, {})} | custom-call | flops 1769472 | bytes 1769472 | tf_op jit(solution)/shard_map/norm_opening/pallas_call | solution.py:407
Async XLA Ops:
  4.1 24.7 %all-to-all-start = ((bf16[8,160,256]{2,1,0:T(8,128)(2,1)}), bf16[8,160,256]{2,1,0:T(8,128)(2,1)}, u32[]{:S(2)}, u32[]{:S(2)}) async-start(bf16[8,160,256]{2,1,0:T(8,128)(2,1)} %tail.1), calls=%async_computation | async-start | bytes 1310720 | tf_op jit(solution)/shard_map/all_to_all | solution.py:426
  30.8 22.1 %all-to-all-start.1 = ((bf16[8,160,256]{2,1,0:T(8,128)(2,1)}), bf16[8,160,256]{2,1,0:T(8,128)(2,1)}, u32[]{:S(2)}, u32[]{:S(2)}) async-start(bf16[8,160,256]{2,1,0:T(8,128)(2,1)} %route.1), calls=%async_computation.1 | async-start | bytes 1310720 | tf_op jit(solution)/shard_map/all_to_all | solution.py:426
  43.9 3.2 %collective-permute-start.2 = (f32[1,384]{1,0:T(1,128)}, f32[1,384]{1,0:T(1,128)}, u32[]{:S(2)}, u32[]{:S(2)}) collective-permute-start(f32[1,384]{1,0:T(1,128)} %get-tuple-element.23.refs_0_), channel_id=1, source_target_pairs={{0,3},{1,2},{2,1},{3,0},{4,7},{5,6},{6,5},{7,4},{8,11},{9,10},{10,... | collective-permute-start | bytes 4616 | tf_op jit(solution)/shard_map/ppermute | solution.py:422
  44.2 3.7 %collective-permute-start.1 = (f32[1,384]{1,0:T(1,128)}, f32[1,384]{1,0:T(1,128)}, u32[]{:S(2)}, u32[]{:S(2)}) collective-permute-start(f32[1,384]{1,0:T(1,128)} %get-tuple-element.23.refs_0_), channel_id=1, source_target_pairs={{0,2},{1,3},{2,0},{3,1},{4,6},{5,7},{6,4},{7,5},{8,10},{9,11},{10,... | collective-permute-start | bytes 4616 | tf_op jit(solution)/shard_map/ppermute | solution.py:422
  45.5 2.4 %collective-permute-start = (f32[1,384]{1,0:T(1,128)}, f32[1,384]{1,0:T(1,128)}, u32[]{:S(2)}, u32[]{:S(2)}) collective-permute-start(f32[1,384]{1,0:T(1,128)} %get-tuple-element.23.refs_0_), channel_id=1, source_target_pairs={{0,1},{1,0},{2,3},{3,2},{4,5},{5,4},{6,7},{7,6},{8,9},{9,8},{10,11... | collective-permute-start | bytes 4616 | tf_op jit(solution)/shard_map/ppermute | solution.py:422
  59.3 3.2 %collective-permute-start.5 = (f32[1,256]{1,0:T(1,128)}, f32[1,256]{1,0:T(1,128)}, u32[]{:S(2)}, u32[]{:S(2)}) collective-permute-start(f32[1,256]{1,0:T(1,128)} %get-tuple-element.30.refs_0_), channel_id=1, source_target_pairs={{0,3},{1,2},{2,1},{3,0},{4,7},{5,6},{6,5},{7,4},{8,11},{9,10},{10,... | collective-permute-start | bytes 3080 | tf_op jit(solution)/shard_map/ppermute | solution.py:422
  60.2 3.7 %collective-permute-start.4 = (f32[1,256]{1,0:T(1,128)}, f32[1,256]{1,0:T(1,128)}, u32[]{:S(2)}, u32[]{:S(2)}) collective-permute-start(f32[1,256]{1,0:T(1,128)} %get-tuple-element.30.refs_0_), channel_id=1, source_target_pairs={{0,2},{1,3},{2,0},{3,1},{4,6},{5,7},{6,4},{7,5},{8,10},{9,11},{10,... | collective-permute-start | bytes 3080 | tf_op jit(solution)/shard_map/ppermute | solution.py:422
  61.7 2.2 %collective-permute-start.3 = (f32[1,256]{1,0:T(1,128)}, f32[1,256]{1,0:T(1,128)}, u32[]{:S(2)}, u32[]{:S(2)}) collective-permute-start(f32[1,256]{1,0:T(1,128)} %get-tuple-element.30.refs_0_), channel_id=1, source_target_pairs={{0,1},{1,0},{2,3},{3,2},{4,5},{5,4},{6,7},{7,6},{8,9},{9,8},{10,11... | collective-permute-start | bytes 3080 | tf_op jit(solution)/shard_map/ppermute | solution.py:422

commit v2 on v1

--- a/solution.py
+++ b/solution.py
@@ -13,11 +13,16 @@
 LANES = 128
 STEP = 256
 WIDE = 512
+SIDE = 4
 BLOCK = 32
 WINDOW = 256
 PACKED = 160
 OPENING = 144
 VMEM_LIMIT = 64 * 1024 * 1024
+
+
+def unfold(picked):
+    return jnp.concatenate([picked[:, i * LANES : (i + 1) * LANES] for i in range(picked.shape[1] // LANES)])
 
 
 def params():
@@ -196,17 +201,15 @@
         lines_ref[...] = spread_taps(all_taps(filt_ref))
         acc[...] = jnp.zeros_like(acc)
 
-    mixed_ref[0:128, :] = jnp.zeros((128, WIDE), BF16)
-
     def pair(index, carry):
         for tile in range(2):
             number = index * 2 + tile
             cols = pl.ds(pl.multiple_of(number * LANES, LANES), LANES)
             base = pl.multiple_of((step * (WIDE // LANES) + number) * per_lane, per_lane)
             matrix = toeplitz(lines_ref[pl.ds(base, per_lane), :])
-            for start in range(128, rows, 2 * BLOCK):
+            for start in range(128, rows, SIDE * BLOCK):
                 windows = []
-                for first in (start, start + BLOCK):
+                for first in range(start, start + SIDE * BLOCK, BLOCK):
                     low = first + BLOCK - WINDOW
                     if low < 0:
                         windows.append(
@@ -216,13 +219,13 @@
                         windows.append(u_ref[low : first + BLOCK, cols])
                 result = jnp.dot(matrix, jnp.concatenate(windows, axis=1), preferred_element_type=F32)
                 picked = pick_groups(result, group_size)
-                filtered = jnp.concatenate([picked[:, :LANES], picked[:, LANES:]])
-                query = query_ref[start - 128 : start - 128 + 2 * BLOCK, cols]
-                row = lax.broadcasted_iota(jnp.int32, (2 * BLOCK, LANES), 0) + start
-                mixed = jnp.where(row < length, query * filtered, 0.0).astype(BF16)
-                mixed_ref[start : start + 2 * BLOCK, cols] = mixed
-                summed = res_ref[start : start + 2 * BLOCK, cols].astype(F32) + mixed.astype(F32)
-                acc[start - 128 : start - 128 + 2 * BLOCK, :] += summed * summed
+                filtered = unfold(picked)
+                here = slice(start - 128, start - 128 + SIDE * BLOCK)
+                row = lax.broadcasted_iota(jnp.int32, filtered.shape, 0) + start
+                mixed = jnp.where(row < length, query_ref[here, cols] * filtered, 0.0).astype(BF16)
+                mixed_ref[here, cols] = mixed
+                summed = res_ref[here, cols].astype(F32) + mixed.astype(F32)
+                acc[here, :] += summed * summed
         return carry
 
     lax.fori_loop(0, WIDE // (2 * LANES), pair, 0)
@@ -240,6 +243,7 @@
     else:
         filter_spec = pl.BlockSpec((filter_rows.shape[0], 16, STEP), lambda p, *_: (0, PACKED // 16 - 1, 0))
     block = pl.BlockSpec((rows, WIDE), lambda p, *_: (0, p))
+    later = pl.BlockSpec((pl.Element(rows - 128), pl.Element(WIDE)), lambda p, *_: (128, p * WIDE))
     return pl.pallas_call(
         functools.partial(main_kernel, group_size),
         grid_spec=pltpu.PrefetchScalarGridSpec(
@@ -248,11 +252,11 @@
             in_specs=[
                 pl.BlockSpec((rows - 128, WIDE), lambda p, *_: (0, p)),
                 block,
-                block,
+                later,
                 filter_spec,
             ],
             out_specs=[
-                block,
+                later,
                 pl.BlockSpec((1, rows - 128), lambda p, *_: (0, 0)),
                 pl.BlockSpec((groups, WINDOW), lambda p, *_: (0, 0)),
             ],
@@ -307,11 +311,12 @@
             base = pl.multiple_of(number * per_lane, per_lane)
             matrix = toeplitz(lines_ref[pl.ds(base, per_lane), :])
             parts = []
-            for first in range(0, 128, 2 * BLOCK):
-                windows = [extended[low : low + WINDOW] for low in (first, first + BLOCK)]
+            for first in range(0, 128, SIDE * BLOCK):
+                lows = range(first, first + SIDE * BLOCK, BLOCK)
+                windows = [extended[low : low + WINDOW] for low in lows]
                 result = jnp.dot(matrix, jnp.concatenate(windows, axis=1), preferred_element_type=F32)
                 picked = pick_groups(result, group_size)
-                parts.append((first, 2 * BLOCK, jnp.concatenate([picked[:, :LANES], picked[:, LANES:]])))
+                parts.append((first, SIDE * BLOCK, unfold(picked)))
             edge = OPENING - 128
             edge_matrix = jnp.concatenate([matrix[g * BLOCK : g * BLOCK + edge] for g in range(per_lane)])
             edge_result = jnp.dot(edge_matrix, extended[128 : 128 + WINDOW], preferred_element_type=F32)

time: 67.6 us -> 67.5 us (level)
  no operation moved by 1% of the time
where the time goes in v2:
time: 67.5 us; the launch traced here: 66.7 us
  Pallas kernels  38.3 us (57%)
  starting transfers between devices  15.7 us (23%)
  waiting for transfers between devices  10.8 us (16%)
  local copies, waits for them, and re-layouts  1.28 us (2%)
    all_to_all x2, starting transfers between devices, exchange(): lax.all_to_all(pieces, 'seq', split_axis=0, concat_axis=0, tiled=True)  11.5 us
    pallas_call x1, Pallas kernels, feature_call(): pl.pallas_call(feature_kernel, grid=(width // WIDE,), in_specs=[blocks[0]...  9.69 us
    pallas_call x1, Pallas kernels, main_call(): pl.pallas_call(functools.partial(main_kernel, group_size), grid_spec=pltp...  8.8 us
    pallas_call x2, Pallas kernels, norm_call(): pl.pallas_call(functools.partial(norm_kernel, channels, first_block, len(...  7.89 us
    pallas_call x1, Pallas kernels, head_call(): pl.pallas_call(functools.partial(head_kernel, group_size), grid_spec=pltp...  6.49 us
    all_to_all x2, waiting for transfers between devices, exchange(): lax.all_to_all(pieces, 'seq', split_axis=0, concat_axis=0, tiled=True)  6.43 us
    ppermute x6, waiting for transfers between devices, swap(): return lax.ppermute(array, axis, [(i, i ^ distance) for i in range(size)])  4.38 us
    ppermute x6, starting transfers between devices, swap(): return lax.ppermute(array, axis, [(i, i ^ distance) for i in range(size)])  4.19 us
  transfers between devices with their start and end apart: 8, of which 5 were waited for; matrix products, arithmetic and copies ran while one was open for 2% of the time, Pallas kernels for 35%

profile of v2, /device:TPU:0, one launch (start us, length us, event | category | flops | bytes accessed | tf_op | source)
XLA Modules:
  0.0 66.7 jit_solution(8396366055947910477)
XLA Ops:
  0.6 3.5 %tail.1 = bf16[8,160,256]{2,1,0:T(8,128)(2,1)} custom-call(bf16[512,2048]{1,0:T(8,128)(2,1)} %q_ref.5, bf16[512,2048]{1,0:T(8,128)(2,1)} %k_ref.5, bf16[512,2048]{1,0:T(8,128)(2,1)} %v_ref.5, bf16[512,2048]{1,0:T(8,128)(2,1)} %k_ref.5, bf16[512,2048]{1,0:T(8,128)(2,1)} %v_ref.5, bf16[3,7,2048]{2,1,0:T(8,128)(2,1)} %taps_ref.5, bf16[16,128]{1,0:T(8,128)(2,1)} %filt_ref.1), custom_call_target="tpu_custom_call" | custom-call | flops 7864320 | bytes 1572864 | tf_op jit(solution)/shard_map/tail/pallas_call | solution.py:76
  4.1 7.3 %all-to-all-start = ((bf16[8,160,256]{2,1,0:T(8,128)(2,1)}), bf16[8,160,256]{2,1,0:T(8,128)(2,1)}, u32[]{:S(2)}, u32[]{:S(2)}) async-start(bf16[8,160,256]{2,1,0:T(8,128)(2,1)} %tail.1), calls=%async_computation | async-start | bytes 1310720 | tf_op jit(solution)/shard_map/all_to_all | solution.py:431
  11.4 1.3 %reshape.7.refs_6_ = bf16[1,2048]{1,0:T(2,128)(2,1)} reshape(bf16[2048]{0:T(1024)(128)(2,1)} %param.15) | data formatting | bytes 8192 | tf_op jit(solution)/shard_map/reshape | solution.py:447
  12.7 9.7 %features.1 = (bf16[512,2048]{1,0:T(8,128)(2,1)}, f32[144,2048]{1,0:T(8,128)}, f32[384,2048]{1,0:T(8,128)}) custom-call(bf16[512,2048]{1,0:T(8,128)(2,1)} %q_ref.5, bf16[512,2048]{1,0:T(8,128)(2,1)} %k_ref.5, bf16[512,2048]{1,0:T(8,128)(2,1)} %v_ref.5, bf16[3,7,2048]{2,1,0:T(8,128)(2,1)} %taps_ref.5), custom_call_target="tpu_custom_call" | custom-call | flops 47185920 | bytes 13631488 | tf_op jit(solution)/shard_map/features/pallas_call | solution.py:126
  22.4 6.4 %all-to-all-done.in_ref.filt_ref = bf16[8,160,256]{2,1,0:T(8,128)(2,1)} async-done(((bf16[8,160,256]{2,1,0:T(8,128)(2,1)}), bf16[8,160,256]{2,1,0:T(8,128)(2,1)}, u32[]{:S(2)}, u32[]{:S(2)}) %all-to-all-start) | async-done | bytes 655392 | tf_op jit(solution)/shard_map/all_to_all | solution.py:431
  28.8 2.0 %route.1 = bf16[8,160,256]{2,1,0:T(8,128)(2,1)} custom-call(s32[8]{0:T(128)} %pred_ref.3, bf16[8,160,256]{2,1,0:T(8,128)(2,1)} %all-to-all-done.in_ref.filt_ref), custom_call_target="tpu_custom_call" | custom-call | bytes 1310720 | tf_op jit(solution)/shard_map/route/pallas_call | solution.py:147
  30.8 4.2 %all-to-all-start.1 = ((bf16[8,160,256]{2,1,0:T(8,128)(2,1)}), bf16[8,160,256]{2,1,0:T(8,128)(2,1)}, u32[]{:S(2)}, u32[]{:S(2)}) async-start(bf16[8,160,256]{2,1,0:T(8,128)(2,1)} %route.1), calls=%async_computation.1 | async-start | bytes 1310720 | tf_op jit(solution)/shard_map/all_to_all | solution.py:431
  35.0 8.8 %conv.1 = (bf16[512,2048]{1,0:T(8,128)(2,1)}, f32[1,384]{1,0:T(1,128)}, f32[128,256]{1,0:T(8,128)}) custom-call(s32[8]{0:T(128)} %len_ref.7, f32[384,2048]{1,0:T(8,128)} %get-tuple-element.20.query_ref, bf16[512,2048]{1,0:T(8,128)(2,1)} %get-tuple-element.21.u_ref, bf16[512,2048]{1,0:T(8,128)(2,1)} %refs_5_.3, bf16[8,160,256]{2,1,0:T(8,128)(2,1)} %all-to-all-done.in_ref.filt_ref), custom_call_target="tpu_custom_call" | custom-call | flops 4294967296 | bytes 12582912 | tf_op jit(solution)/shard_map/conv/pallas_call | solution.py:247
  43.8 0.3 collective-permute-start.2
  44.0 1.3 %collective-permute-start.1 = (f32[1,384]{1,0:T(1,128)}, f32[1,384]{1,0:T(1,128)}, u32[]{:S(2)}, u32[]{:S(2)}) collective-permute-start(f32[1,384]{1,0:T(1,128)} %get-tuple-element.23.refs_0_), channel_id=1, source_target_pairs={{0,2},{1,3},{2,0},{3,1},{4,6},{5,7},{6,4},{7,5},{8,10},{9,11},{10,... | collective-permute-start | bytes 4616 | tf_op jit(solution)/shard_map/ppermute | solution.py:427
  45.3 0.3 collective-permute-start
  45.6 1.3 %collective-permute-done.2.refs_3_ = f32[1,384]{1,0:T(1,128)} collective-permute-done((f32[1,384]{1,0:T(1,128)}, f32[1,384]{1,0:T(1,128)}, u32[]{:S(2)}, u32[]{:S(2)}) %collective-permute-start.2) | collective-permute-done | bytes 1568 | tf_op jit(solution)/shard_map/ppermute | solution.py:427
  46.9 0.8 %collective-permute-done.1.refs_2_ = f32[1,384]{1,0:T(1,128)} collective-permute-done((f32[1,384]{1,0:T(1,128)}, f32[1,384]{1,0:T(1,128)}, u32[]{:S(2)}, u32[]{:S(2)}) %collective-permute-start.1) | collective-permute-done | bytes 1568 | tf_op jit(solution)/shard_map/ppermute | solution.py:427
  47.8 0.0 collective-permute-done.refs_1_
  47.8 4.9 %norm.1.refs_7_ = bf16[512,2048]{1,0:T(8,128)(2,1)} custom-call(s32[8]{0:T(128)} %len_ref.7, f32[1,384]{1,0:T(1,128)} %get-tuple-element.23.refs_0_, f32[1,384]{1,0:T(1,128)} %collective-permute-done.refs_1_, f32[1,384]{1,0:T(1,128)} %collective-permute-done.1.refs_2_, f32[1,384]{1,0:T(1,128)} %collective-permute-done.2.refs_3_, ...), custom_call_target="tpu_custom_call" | custom-call | flops 4718592 | bytes 4718592 | tf_op jit(solution)/shard_map/norm/pallas_call | solution.py:412
  52.7 0.0 all-to-all-done.1.held
  52.7 6.5 %head.1 = (bf16[512,2048]{1,0:T(8,128)(2,1)}, f32[1,256]{1,0:T(1,128)}) custom-call(s32[8]{0:T(128)} %pred_ref.3, s32[8]{0:T(128)} %len_ref.7, bf16[8,160,256]{2,1,0:T(8,128)(2,1)} %all-to-all-done.1.held, f32[144,2048]{1,0:T(8,128)} %get-tuple-element.27.query_ref, bf16[512,2048]{1,0:T(8,128)(2,1)} %q_ref.5, ...), custom_call_target="tpu_custom_call", output_to_operand_aliasing={{0}: (11, {})} | custom-call | flops 1073741824 | bytes 3145728 | tf_op jit(solution)/shard_map/head/pallas_call | solution.py:347
  59.2 0.8 %collective-permute-start.5 = (f32[1,256]{1,0:T(1,128)}, f32[1,256]{1,0:T(1,128)}, u32[]{:S(2)}, u32[]{:S(2)}) collective-permute-start(f32[1,256]{1,0:T(1,128)} %get-tuple-element.30.refs_0_), channel_id=1, source_target_pairs={{0,3},{1,2},{2,1},{3,0},{4,7},{5,6},{6,5},{7,4},{8,11},{9,10},{10,... | collective-permute-start | bytes 3080 | tf_op jit(solution)/shard_map/ppermute | solution.py:427
  60.0 1.5 %collective-permute-start.4 = (f32[1,256]{1,0:T(1,128)}, f32[1,256]{1,0:T(1,128)}, u32[]{:S(2)}, u32[]{:S(2)}) collective-permute-start(f32[1,256]{1,0:T(1,128)} %get-tuple-element.30.refs_0_), channel_id=1, source_target_pairs={{0,2},{1,3},{2,0},{3,1},{4,6},{5,7},{6,4},{7,5},{8,10},{9,11},{10,... | collective-permute-start | bytes 3080 | tf_op jit(solution)/shard_map/ppermute | solution.py:427
  61.5 0.0 collective-permute-start.3
  61.5 0.9 %collective-permute-done.5.refs_3_ = f32[1,256]{1,0:T(1,128)} collective-permute-done((f32[1,256]{1,0:T(1,128)}, f32[1,256]{1,0:T(1,128)}, u32[]{:S(2)}, u32[]{:S(2)}) %collective-permute-start.5) | collective-permute-done | bytes 1056 | tf_op jit(solution)/shard_map/ppermute | solution.py:427
  62.4 1.4 %collective-permute-done.4.refs_2_ = f32[1,256]{1,0:T(1,128)} collective-permute-done((f32[1,256]{1,0:T(1,128)}, f32[1,256]{1,0:T(1,128)}, u32[]{:S(2)}, u32[]{:S(2)}) %collective-permute-start.4) | collective-permute-done | bytes 1056 | tf_op jit(solution)/shard_map/ppermute | solution.py:427
  63.7 0.0 collective-permute-done.3.refs_1_
  63.7 3.0 %norm_opening.1 = bf16[512,2048]{1,0:T(8,128)(2,1)} custom-call(s32[8]{0:T(128)} %len_ref.7, f32[1,256]{1,0:T(1,128)} %get-tuple-element.30.refs_0_, f32[1,256]{1,0:T(1,128)} %collective-permute-done.3.refs_1_, f32[1,256]{1,0:T(1,128)} %collective-permute-done.4.refs_2_, f32[1,256]{1,0:T(1,128)} %collective-permute-done.5.refs_3_, ...), custom_call_target="tpu_custom_call", output_to_operand_aliasing={{}: (8, {})} | custom-call | flops 1769472 | bytes 1769472 | tf_op jit(solution)/shard_map/norm_opening/pallas_call | solution.py:412
Async XLA Ops:
  4.1 24.7 %all-to-all-start = ((bf16[8,160,256]{2,1,0:T(8,128)(2,1)}), bf16[8,160,256]{2,1,0:T(8,128)(2,1)}, u32[]{:S(2)}, u32[]{:S(2)}) async-start(bf16[8,160,256]{2,1,0:T(8,128)(2,1)} %tail.1), calls=%async_computation | async-start | bytes 1310720 | tf_op jit(solution)/shard_map/all_to_all | solution.py:431
  30.8 21.9 %all-to-all-start.1 = ((bf16[8,160,256]{2,1,0:T(8,128)(2,1)}), bf16[8,160,256]{2,1,0:T(8,128)(2,1)}, u32[]{:S(2)}, u32[]{:S(2)}) async-start(bf16[8,160,256]{2,1,0:T(8,128)(2,1)} %route.1), calls=%async_computation.1 | async-start | bytes 1310720 | tf_op jit(solution)/shard_map/all_to_all | solution.py:431
  43.8 3.2 %collective-permute-start.2 = (f32[1,384]{1,0:T(1,128)}, f32[1,384]{1,0:T(1,128)}, u32[]{:S(2)}, u32[]{:S(2)}) collective-permute-start(f32[1,384]{1,0:T(1,128)} %get-tuple-element.23.refs_0_), channel_id=1, source_target_pairs={{0,3},{1,2},{2,1},{3,0},{4,7},{5,6},{6,5},{7,4},{8,11},{9,10},{10,... | collective-permute-start | bytes 4616 | tf_op jit(solution)/shard_map/ppermute | solution.py:427
  44.0 3.7 %collective-permute-start.1 = (f32[1,384]{1,0:T(1,128)}, f32[1,384]{1,0:T(1,128)}, u32[]{:S(2)}, u32[]{:S(2)}) collective-permute-start(f32[1,384]{1,0:T(1,128)} %get-tuple-element.23.refs_0_), channel_id=1, source_target_pairs={{0,2},{1,3},{2,0},{3,1},{4,6},{5,7},{6,4},{7,5},{8,10},{9,11},{10,... | collective-permute-start | bytes 4616 | tf_op jit(solution)/shard_map/ppermute | solution.py:427
  45.3 2.4 %collective-permute-start = (f32[1,384]{1,0:T(1,128)}, f32[1,384]{1,0:T(1,128)}, u32[]{:S(2)}, u32[]{:S(2)}) collective-permute-start(f32[1,384]{1,0:T(1,128)} %get-tuple-element.23.refs_0_), channel_id=1, source_target_pairs={{0,1},{1,0},{2,3},{3,2},{4,5},{5,4},{6,7},{7,6},{8,9},{9,8},{10,11... | collective-permute-start | bytes 4616 | tf_op jit(solution)/shard_map/ppermute | solution.py:427
  59.2 3.2 %collective-permute-start.5 = (f32[1,256]{1,0:T(1,128)}, f32[1,256]{1,0:T(1,128)}, u32[]{:S(2)}, u32[]{:S(2)}) collective-permute-start(f32[1,256]{1,0:T(1,128)} %get-tuple-element.30.refs_0_), channel_id=1, source_target_pairs={{0,3},{1,2},{2,1},{3,0},{4,7},{5,6},{6,5},{7,4},{8,11},{9,10},{10,... | collective-permute-start | bytes 3080 | tf_op jit(solution)/shard_map/ppermute | solution.py:427
  60.0 3.7 %collective-permute-start.4 = (f32[1,256]{1,0:T(1,128)}, f32[1,256]{1,0:T(1,128)}, u32[]{:S(2)}, u32[]{:S(2)}) collective-permute-start(f32[1,256]{1,0:T(1,128)} %get-tuple-element.30.refs_0_), channel_id=1, source_target_pairs={{0,2},{1,3},{2,0},{3,1},{4,6},{5,7},{6,4},{7,5},{8,10},{9,11},{10,... | collective-permute-start | bytes 3080 | tf_op jit(solution)/shard_map/ppermute | solution.py:427
  61.5 2.2 %collective-permute-start.3 = (f32[1,256]{1,0:T(1,128)}, f32[1,256]{1,0:T(1,128)}, u32[]{:S(2)}, u32[]{:S(2)}) collective-permute-start(f32[1,256]{1,0:T(1,128)} %get-tuple-element.30.refs_0_), channel_id=1, source_target_pairs={{0,1},{1,0},{2,3},{3,2},{4,5},{5,4},{6,7},{7,6},{8,9},{9,8},{10,11... | collective-permute-start | bytes 3080 | tf_op jit(solution)/shard_map/ppermute | solution.py:427
